TPU v7x, 256 devices: a whole 4x4x8 slice. The times are simulated.
256 devices in a mesh: dp: 16 (over z, x_lo), token: 16 (over y, x_hi, core).
Axes of the slice: x: 4 (x_hi: 2, x_lo: 2; x = x_hi * 2 + x_lo), y: 4, z: 8, core: 2. Of those that a mesh axis runs over, the one named last changes fastest.
Arguments:
- tokens: bfloat16 [1024, 16, 1536], P('dp', 'token'), may hold values from -180 to 180
- grad_out: bfloat16 [1024, 16, 1536], P('dp', 'token'), may hold values from -36 to 36
- gain: float32 [16, 1536], P('token'), may hold values from 0.1 to 1.9
- w_gate: bfloat16 [16, 1536, 6144], P('token', None, 'dp'), may hold values from -0.15625 to 0.15625
- w_up: bfloat16 [16, 1536, 6144], P('token', None, 'dp'), may hold values from -0.15625 to 0.15625
- w_down: bfloat16 [16, 6144, 1536], P('token', 'dp'), may hold values from -0.078125 to 0.078125
Outputs:
- d_tokens: bfloat16 [1024, 16, 1536], P('dp', 'token')
- d_w_gate: bfloat16 [16, 1536, 6144], P('token', None, 'dp')
- d_w_up: bfloat16 [16, 1536, 6144], P('token', None, 'dp')
- d_w_down: bfloat16 [16, 6144, 1536], P('token', 'dp')
- d_gain: float32 [16, 1536], P('token')
All inputs are finite; a program needn't handle non-finite values.
Results may differ from a plain program's by a relative error of at most 0.023.
Values may be sent and summed in bfloat16 or wider, within the bound.
No kernel may reach another device: no remote copies, remote signals or barrier semaphores. Data moves between devices by JAX's collectives and lax.ppermute only.
A program may use at most 128 MiB of HBM per device.

v0:
```python
import jax
import jax.numpy as jnp
from jax import lax
from jax.experimental import pallas as pl
from jax.experimental.pallas import tpu as pltpu
from jax.sharding import PartitionSpec as P

BF = jnp.bfloat16
F32 = jnp.float32
VMEM = 40 * 1024 * 1024
ROWS_IN = ((0,), (0,))
COLUMNS_OUT = ((1,), (0,))
COLUMNS_IN = ((1,), (1,))
HBM = pl.BlockSpec(memory_space=pl.ANY)


def moves(size):
    ring = size // 2

    def swap(partner):
        pairs = [(z * 2 + x, (partner(z) % ring) * 2 + x) for z in range(ring) for x in range(2)]
        return lambda block: lax.ppermute(block, "dp", pairs)

    first = swap(lambda z: z + 1 if z % 2 == 0 else z - 1)
    other = swap(lambda z: z - 1 if z % 2 == 0 else z + 1)
    return first, other, lambda block: lax.ppermute(block, "dp", [(at, at ^ 1) for at in range(size)])


def tie(values, others):
    return lax.optimization_barrier((tuple(values), tuple(others)))[0]


def opposite(block, size):
    return lax.ppermute(block, "dp", [(at, (at + size // 2) % size) for at in range(size)])


def dot(a, b, dims):
    return lax.dot_general(a, b, (dims, ((), ())), preferred_element_type=F32)


def kernel(body, shapes, args, name, flops=0, specs=None, scratch=()):
    outs = tuple(jax.ShapeDtypeStruct(shape, kind) for shape, kind in shapes)
    moved = sum(a.size * a.dtype.itemsize for a in args) + sum(o.size * o.dtype.itemsize for o in outs)
    whole = pl.BlockSpec(memory_space=pltpu.VMEM)
    return pl.pallas_call(
        body,
        out_shape=outs,
        in_specs=[whole] * len(args) if specs is None else specs,
        out_specs=tuple(whole for _ in outs),
        scratch_shapes=list(scratch),
        compiler_params=pltpu.CompilerParams(vmem_limit_bytes=VMEM),
        cost_estimate=pl.CostEstimate(flops=flops, bytes_accessed=moved, transcendentals=0),
        name=name,
    )(*args)


def put_heads(ref, whole):
    size = ref.shape[2]
    for head in range(ref.shape[0]):
        ref[head] = whole[:, head * size : (head + 1) * size].astype(BF)


def take_heads(ref):
    return jnp.concatenate([ref[head].astype(F32) for head in range(ref.shape[0])], axis=1)


def split_heads(source, heads):
    rows, features = source.shape

    def body(source_ref, out_ref):
        put_heads(out_ref, source_ref[...].astype(F32))

    return kernel(body, [((heads, rows, features // heads), BF)], [source], "split_heads")[0]


def normalize(arrived, tokens, gain):
    rows, features = tokens.shape

    def body(arrived_ref, tokens_ref, gain_ref, hidden_ref, normed_ref, scale_ref):
        summed = tokens_ref[...].astype(F32) + take_heads(arrived_ref)
        scale = lax.rsqrt(jnp.mean(summed * summed, axis=-1, keepdims=True) + 1e-06)
        normed = summed * scale
        hidden_ref[...] = (normed * gain_ref[...]).astype(BF)
        normed_ref[...] = normed
        scale_ref[...] = jnp.broadcast_to(scale, (rows, 128))

    shapes = [((rows, features), BF), ((rows, features), F32), ((rows, 128), F32)]
    return kernel(body, shapes, [arrived, tokens, gain], "normalize", flops=30 * 10**9)


def token_gradient(own, arrived, around, grad_out, normed, scale, gain, heads):
    rows, features = grad_out.shape

    def body(own_ref, a_ref, b_ref, c_ref, d_ref, near_ref, grad_ref, normed_ref, scale_ref, gain_ref, sum_ref, heads_ref, total_ref):
        d_hidden = own_ref[...].astype(F32)
        for ref in (a_ref, b_ref, c_ref, d_ref):
            d_hidden = d_hidden + ref[:rows, :].astype(F32)
        scaled = d_hidden * gain_ref[...]
        normed = normed_ref[...]
        mean = jnp.mean(scaled * normed, axis=-1, keepdims=True)
        d_summed = grad_ref[...].astype(F32) + scale_ref[:, :1] * (scaled - normed * mean)
        sum_ref[...] = d_summed
        put_heads(heads_ref, d_summed)
        total_ref[...] = near_ref[...] + word_sum(a_ref[rows:, :].astype(F32)) + word_sum(b_ref[rows:, :].astype(F32))

    shapes = [((rows, features), F32), ((heads, rows, features // heads), BF), ((1, features), F32)]
    return kernel(body, shapes, [own, *arrived, around, grad_out, normed, scale, gain], "token_gradient")


def total_gain(one, two):
    def body(one_ref, two_ref, out_ref):
        out_ref[...] = one_ref[...] + two_ref[...]

    return kernel(body, [(one.shape, F32)], [one, two], "total_gain", flops=10**9)[0]


def add_heads(d_summed, arrived):
    def body(sum_ref, arrived_ref, out_ref):
        out_ref[...] = (sum_ref[...] + take_heads(arrived_ref)).astype(BF)

    return kernel(body, [(d_summed.shape, BF)], [d_summed, arrived], "add_heads")[0]


def join_two(one, two):
    rows, features = one.shape

    def body(one_ref, two_ref, out_ref, sems):
        copies = [pltpu.make_async_copy(ref, out_ref.at[pl.ds(at * rows, rows)], sems.at[at]) for at, ref in enumerate((one_ref, two_ref))]
        for copy in copies:
            copy.start()
        for copy in copies:
            copy.wait()

    return kernel(body, [((2 * rows, features), BF)], [one, two], "join_two", flops=20 * 10**9, specs=[HBM] * 2, scratch=[pltpu.SemaphoreType.DMA((2,))])[0]


def feed_forward(blocks, grads, w_gate, w_up, w_down):
    rows = blocks[0][0].shape[0]
    flat = [block for two in blocks for block in two]
    count = len(flat) * rows
    features, units = w_gate.shape
    half = rows // 2
    alone, paired = len(blocks) % 2, len(blocks) // 2
    n_in = len(flat) + len(grads) + 3

    def body(*refs):
        row_refs, grad_refs = refs[: len(flat)], refs[len(flat) : n_in - 3]
        wg_ref, wu_ref, wd_ref = refs[n_in - 3 : n_in]
        row_ref, grad_ref, act_ref, dg_ref, du_ref, gain_ref = refs[n_in : n_in + 6]
        part_refs = refs[n_in + 6 :]
        for whole, pieces in ((row_ref, row_refs), (grad_ref, grad_refs)):
            at = 0
            for piece in pieces:
                whole[at : at + piece.shape[0], :] = piece[...]
                at += piece.shape[0]
        row = row_ref[...]
        gate_out = dot(row, wg_ref[...], COLUMNS_OUT)
        up_out = dot(row, wu_ref[...], COLUMNS_OUT)
        d_activation = dot(grad_ref[...], wd_ref[...], COLUMNS_IN)
        sigmoid_gate = jax.nn.sigmoid(gate_out)
        silu_gate = gate_out * sigmoid_gate
        act_ref[...] = (silu_gate * up_out).astype(BF)
        silu_slope = sigmoid_gate * (1.0 + gate_out * (1.0 - sigmoid_gate))
        d_gate_pre = (d_activation * up_out * silu_slope).astype(BF)
        d_up_pre = (d_activation * silu_gate).astype(BF)
        dg_ref[...] = d_gate_pre
        du_ref[...] = d_up_pre
        part = dot(d_gate_pre, wg_ref[...], COLUMNS_IN) + dot(d_up_pre, wu_ref[...], COLUMNS_IN)
        gain_ref[...] = jnp.sum(part * row_ref[...].astype(F32), axis=0, keepdims=True)
        part = part.astype(BF)
        at, out = 0, iter(part_refs)
        for _ in range(alone):
            next(out)[...] = part[at : at + rows]
            next(out)[...] = part[at + rows : at + 2 * rows]
            at += 2 * rows
        for _ in range(paired):
            up, up_side, dn, dn_side = (part[at + i * rows : at + (i + 1) * rows] for i in range(4))
            for whole in (up, dn):
                next(out)[...] = whole
            for piece in (up_side[:half], dn_side[:half]):
                next(out)[...] = piece
            high = next(out)
            high[:half] = up_side[half:]
            high[half:] = dn_side[half:]
            at += 4 * rows

    wide, thin, piece, short = ((count, features), BF), ((count, units), BF), ((rows, features), BF), ((half, features), BF)
    shapes = [wide, wide, thin, thin, thin, ((1, features), F32)] + [piece] * (2 * alone) + [piece, piece, short, short, piece] * paired
    return kernel(body, shapes, [*flat, *grads, w_gate, w_up, w_down], "feed_forward", flops=10 * count * features * units)


def two_words(value):
    high = value.astype(BF).astype(F32)
    at = lax.broadcasted_iota(jnp.int32, (16, value.shape[1]), 0)
    return jnp.where(at == 0, high, jnp.where(at == 1, value - high, 0.0))


def word_sum(rows):
    return jnp.sum(rows, axis=0, keepdims=True)


def add_step(step, args, widths):
    features = args[0].shape[1]
    count = len(args)

    def body(*refs):
        for out, parts in zip(refs[count:], step([ref[...].astype(F32) for ref in refs[:count]])):
            at = 0
            for part in parts:
                out[at : at + part.shape[0], :] = part.astype(out.dtype)
                at += part.shape[0]

    shapes = [((1, features), F32) if width is F32 else ((width, features), BF) for width in widths]
    return kernel(body, shapes, args, "add_step")


def weight_gradient(lefts, rights, name):
    count, shape = len(lefts), (lefts[0].shape[1], rights[0].shape[1])

    def body(*refs):
        total = dot(refs[0][...], refs[count][...], ROWS_IN)
        for at in range(1, count):
            total = total + dot(refs[at][...], refs[count + at][...], ROWS_IN)
        refs[-1][...] = total.astype(BF)

    rows = sum(left.shape[0] for left in lefts)
    return kernel(body, [(shape, BF)], [*lefts, *rights], name, flops=2 * rows * shape[0] * shape[1])[0]


def shards(tokens, grad_out, gain, w_gate, w_up, w_down):
    rows = tokens.shape[0]
    half = rows // 2
    wide = rows + half
    heads, size = lax.axis_size("token"), lax.axis_size("dp")
    first, other, pair = moves(size)
    w_gate, w_up, w_down = w_gate[0], w_up[0], w_down[0]

    def exchange(blocks):
        return lax.all_to_all(blocks, "token", split_axis=0, concat_axis=0, tiled=True)

    tokens, grad_out = tokens[:, 0], grad_out[:, 0]
    g_s0 = pair(grad_out)
    mixed_in = exchange(split_heads(tokens, heads))
    hidden_in, normed, scale = normalize(mixed_in, tokens, gain)
    g0 = join_two(grad_out, g_s0)

    u1, d1, s0 = first(hidden_in), other(hidden_in), pair(hidden_in)
    g_u1, g_d1 = first(g0), other(g0)
    u2, d2, s_u1, s_d1 = first(d1), other(u1), pair(u1), pair(d1)
    g_u2, g_d2 = first(g_d1), other(g_u1)
    u2, d2 = tie([u2, d2], [s0])
    u3, d3, s_u2, s_d2 = first(d2), other(u2), pair(u2), pair(d2)
    g_u3, g_d3 = first(g_d2), other(g_u2)
    u3, d3 = tie([u3, d3], [s_u1, s_d1, s_u2, s_d2])
    s_u3, s_d3, far = pair(u3), pair(d3), first(d3)
    g_far = other(g_u3)
    near = feed_forward([(hidden_in, s0), (u1, s_u1), (d1, s_d1)], [g0, g_u1, g_d1], w_gate, w_up, w_down)
    second = feed_forward([(u2, s_u2), (d2, s_d2)], [g_u2, g_d2], w_gate, w_up, w_down)
    s_u3, s_d3 = tie([s_u3, s_d3], [near[6], second[6], far])
    third = feed_forward([(u3, s_u3), (d3, s_d3)], [g_u3, g_d3], w_gate, w_up, w_down)

    own, own_side, p_u1, p_d1, low_u1, low_d1, high1 = near[6:]
    p_u2, p_d2, low_u2, low_d2, high2 = second[6:]
    p_u3, p_d3, low_u3, low_d3, high3 = third[6:]

    def first_sums(v):
        a, b, c, up, dn, up_low, dn_low = v
        return [(up[:half], up[half:] + c[:half], up_low + a), (dn[:half], dn[half:] + c[half:], dn_low + b)]

    def second_sums(v):
        a, b, c, up, dn, up_low, dn_low, p_far, got, one, two = v
        spare = two_words(one + two)
        go_up = (up[:half] + a[:half], up[half:] + a[half:rows] + c[:half], up_low + a[rows:], spare)
        go_dn = (dn[:half] + b[:half], dn[half:] + b[half:rows] + c[half:], dn_low + b[rows:], spare)
        return [go_up, go_dn, (p_far + got,)]

    def last_sums(v):
        a, b, c, up, dn, side, one, two = v
        go_up = (up[:half] + a[:half], up[half:] + a[half:rows] + c[:half], a[wide:])
        go_dn = (dn[:half] + b[:half], dn[half:] + b[half:rows] + c[half:], b[wide:])
        around = one + two + word_sum(a[wide:]) + word_sum(b[wide:])
        return [go_up, go_dn, (side[:half] + a[rows:wide] + b[rows:wide], side[half:]), (around,)]

    a, b, c, s_far = other(low_d3), first(low_u3), pair(high3), pair(far)
    go_up, go_dn = add_step(first_sums, [a, b, c, p_u3, p_d3, low_u2, low_d2], (wide, wide))
    a, b, c = other(go_dn), first(go_up), pair(high2)
    (s_far,) = tie([s_far], [go_up])
    fourth = feed_forward([(far, s_far)], [g_far], w_gate, w_up, w_down)
    groups = (near, second, third, fourth)
    part = sum(group[5] for group in groups) / gain
    p_far, p_far_side = fourth[6:]
    part_side, got = pair(part), pair(p_far_side)
    d_w_down = weight_gradient([group[2] for group in groups], [group[1] for group in groups], "d_w_down")
    a, b, c = tie([a, b, c], [part_side, got, d_w_down])
    sums = [a, b, c, p_u2, p_d2, low_u1, low_d1, p_far, got, part, part_side]
    go_up, go_dn, straight = add_step(second_sums, sums, (wide + 16, wide + 16, rows))
    a, b, c = other(go_dn), first(go_up), pair(high1)
    row_parts = tie([group[0] for group in groups], [go_up])
    d_w_gate = weight_gradient(row_parts, [group[3] for group in groups], "d_w_gate")
    a, b, c = tie([a, b, c], [d_w_gate])
    sums = [a, b, c, p_u1, p_d1, own_side, part, part_side]
    go_up, go_dn, go_side, around = add_step(last_sums, sums, (rows + 16, rows + 16, rows, F32))
    straight = opposite(straight, size)
    row_parts = tie([group[0] for group in groups], [go_up, straight])
    d_w_up = weight_gradient(row_parts, [group[4] for group in groups], "d_w_up")
    arrived = tie([other(go_dn), first(go_up), pair(go_side), straight], [d_w_up])

    d_summed, outgoing, five = token_gradient(own, arrived, around, grad_out, normed, scale, gain, heads)
    (around,) = tie([around], [outgoing])
    d_gain = total_gain(five, opposite(around, size))
    d_tokens = add_heads(d_summed, exchange(outgoing))
    return d_tokens[:, None], d_w_gate[None], d_w_up[None], d_w_down[None], d_gain


def solution(mesh):
    placed = (
        P("dp", "token", None),
        P("dp", "token", None),
        P("token", None),
        P("token", None, "dp"),
        P("token", None, "dp"),
        P("token", "dp", None),
    )
    return jax.shard_map(
        shards,
        mesh=mesh,
        in_specs=placed,
        out_specs=(
            P("dp", "token", None),
            P("token", None, "dp"),
            P("token", None, "dp"),
            P("token", "dp", None),
            P("token", None),
        ),
        check_vma=False,
    )
```

profile of v0, /device:TPU:1, one launch (start us, length us, event | category | flops | bytes accessed | tf_op | source)
XLA Modules:
  0.0 135.2 jit_solution(15529024202527726610)
XLA Ops:
  0.6 2.1 %collective-permute-start.5 = (bf16[64,1536]{1,0:T(8,128)(2,1)}, bf16[64,1536]{1,0:T(8,128)(2,1)S(1)}, u32[]{:S(2)}, u32[]{:S(2)}) collective-permute-start(bf16[64,1536]{1,0:T(8,128)(2,1)} %bitcast.23), channel_id=1, source_target_pairs={{0,16},{16,0},{32,48},{48,32},{64,80},{80,64},{96,112},{112,96},{1... | collective-permute-start | bytes 589832 | tf_op jit(solution)/shard_map/ppermute | solution.py:26
  4.6 7.6 %all-to-all-start = ((bf16[16,64,96]{2,1,0:T(8,128)(2,1)}), bf16[16,64,96]{2,1,0:T(8,128)(2,1)}, u32[]{:S(2)}, u32[]{:S(2)}) async-start(bf16[16,64,96]{2,1,0:T(8,128)(2,1)} %split_heads.1), calls=%async_computation | async-start | bytes 524288 | tf_op jit(solution)/shard_map/all_to_all | solution.py:239
  16.1 4.7 %collective-permute-start.7 = (bf16[128,1536]{1,0:T(8,128)(2,1)}, bf16[128,1536]{1,0:T(8,128)(2,1)}, u32[]{:S(2)}, u32[]{:S(2)}) collective-permute-start(bf16[128,1536]{1,0:T(8,128)(2,1)} %join_two.1.refs_6_), channel_id=1, source_target_pairs={{0,224},{16,240},{32,64},{48,80},{64,32},{80,48},{96,128},{112,144... | collective-permute-start | bytes 1179656 | tf_op jit(solution)/shard_map/ppermute | solution.py:22
  23.1 5.7 %collective-permute-start.3 = (bf16[64,1536]{1,0:T(8,128)(2,1)S(1)}, bf16[64,1536]{1,0:T(8,128)(2,1)S(1)}, u32[]{:S(2)}, u32[]{:S(2)}) collective-permute-start(bf16[64,1536]{1,0:T(8,128)(2,1)S(1)} %get-tuple-element.89.refs_0_), channel_id=1, source_target_pairs={{0,224},{16,240},{32,64},{48,80},{64,32},{80,48},{96,128},{112,144... | collective-permute-start | bytes 589832 | tf_op jit(solution)/shard_map/ppermute | solution.py:22
  28.8 5.6 %collective-permute-done.3.refs_4_ = bf16[64,1536]{1,0:T(8,128)(2,1)S(1)} collective-permute-done((bf16[64,1536]{1,0:T(8,128)(2,1)S(1)}, bf16[64,1536]{1,0:T(8,128)(2,1)S(1)}, u32[]{:S(2)}, u32[]{:S(2)}) %collective-permute-start.3) | collective-permute-done | bytes 196640 | tf_op jit(solution)/shard_map/ppermute | solution.py:22
  34.4 2.4 %collective-permute-start.9 = (bf16[64,1536]{1,0:T(8,128)(2,1)S(1)}, bf16[64,1536]{1,0:T(8,128)(2,1)S(1)}, u32[]{:S(2)}, u32[]{:S(2)}) collective-permute-start(bf16[64,1536]{1,0:T(8,128)(2,1)S(1)} %collective-permute-done.1.refs_2_), channel_id=1, source_target_pairs={{0,224},{16,240},{32,64},{48,80},{64,32},{80,48},{96,128},{112,144... | collective-permute-start | bytes 589832 | tf_op jit(solution)/shard_map/ppermute | solution.py:22
  37.3 2.5 %collective-permute-done.8.refs_0_ = bf16[64,1536]{1,0:T(8,128)(2,1)S(1)} collective-permute-done((bf16[64,1536]{1,0:T(8,128)(2,1)S(1)}, bf16[64,1536]{1,0:T(8,128)(2,1)S(1)}, u32[]{:S(2)}, u32[]{:S(2)}) %collective-permute-start.8) | collective-permute-done | bytes 196640 | tf_op jit(solution)/shard_map/ppermute | solution.py:22
  42.1 2.4 %collective-permute-start.11 = (bf16[64,1536]{1,0:T(8,128)(2,1)S(1)}, bf16[64,1536]{1,0:T(8,128)(2,1)S(1)}, u32[]{:S(2)}, u32[]{:S(2)}) collective-permute-start(bf16[64,1536]{1,0:T(8,128)(2,1)S(1)} %collective-permute-done.8.refs_0_), channel_id=1, source_target_pairs={{0,224},{16,240},{32,64},{48,80},{64,32},{80,48},{96,128},{112,144... | collective-permute-start | bytes 589832 | tf_op jit(solution)/shard_map/ppermute | solution.py:22
  44.5 2.2 %collective-permute-done.4.refs_5_ = bf16[64,1536]{1,0:T(8,128)(2,1)S(1)} collective-permute-done((bf16[64,1536]{1,0:T(8,128)(2,1)S(1)}, bf16[64,1536]{1,0:T(8,128)(2,1)S(1)}, u32[]{:S(2)}, u32[]{:S(2)}) %collective-permute-start.4) | collective-permute-done | bytes 196640 | tf_op jit(solution)/shard_map/ppermute | solution.py:26
  46.7 5.7 %collective-permute-done.10.refs_0_ = bf16[64,1536]{1,0:T(8,128)(2,1)S(1)} collective-permute-done((bf16[64,1536]{1,0:T(8,128)(2,1)S(1)}, bf16[64,1536]{1,0:T(8,128)(2,1)S(1)}, u32[]{:S(2)}, u32[]{:S(2)}) %collective-permute-start.10) | collective-permute-done | bytes 196640 | tf_op jit(solution)/shard_map/ppermute | solution.py:22
  52.7 2.4 %collective-permute-start.20 = (bf16[128,1536]{1,0:T(8,128)(2,1)S(1)}, bf16[128,1536]{1,0:T(8,128)(2,1)S(1)}, u32[]{:S(2)}, u32[]{:S(2)}) collective-permute-start(bf16[128,1536]{1,0:T(8,128)(2,1)S(1)} %collective-permute-done.16.refs_4_), channel_id=1, source_target_pairs={{0,224},{16,240},{32,64},{48,80},{64,32},{80,48},{96,128},{112,144... | collective-permute-start | bytes 1179656 | tf_op jit(solution)/shard_map/ppermute | solution.py:22
  59.4 4.6 %feed_forward.4 = (bf16[384,1536]{1,0:T(8,128)(2,1)S(1)}, bf16[384,1536]{1,0:T(8,128)(2,1)S(1)}, bf16[384,384]{1,0:T(8,128)(2,1)S(1)}, bf16[384,384]{1,0:T(8,128...) custom-call(bf16[64,1536]{1,0:T(8,128)(2,1)S(1)} %get-tuple-element., ...), custom_call_target="tpu_custom_call" | custom-call | flops 2264924160 | bytes 10328064 | tf_op jit(solution)/shard_map/feed_forward/pallas_call | solution.py:45
  65.7 2.3 %feed_forward.5 = (bf16[256,1536]{1,0:T(8,128)(2,1)S(1)}, bf16[256,1536]{1,0:T(8,128)(2,1)S(1)}, bf16[256,384]{1,0:T(8,128)(2,1)S(1)}, bf16[256,384]{1,0:T(8,128...) custom-call(bf16[64,1536]{1,0:T(8,128)(2,1)S(1)} %collective-permute, ...), custom_call_target="tpu_custom_call" | custom-call | flops 1509949440 | bytes 8067072 | tf_op jit(solution)/shard_map/feed_forward/pallas_call | solution.py:45
  68.1 2.3 %feed_forward.6 = (bf16[256,1536]{1,0:T(8,128)(2,1)S(1)}, bf16[256,1536]{1,0:T(8,128)(2,1)S(1)}, bf16[256,384]{1,0:T(8,128)(2,1)S(1)}, bf16[256,384]{1,0:T(8,128...) custom-call(bf16[64,1536]{1,0:T(8,128)(2,1)S(1)} %collective-permute, ...), custom_call_target="tpu_custom_call" | custom-call | flops 1509949440 | bytes 8067072 | tf_op jit(solution)/shard_map/feed_forward/pallas_call | solution.py:45
  73.1 4.2 %collective-permute-done.21.refs_0_ = bf16[32,1536]{1,0:T(8,128)(2,1)S(1)} collective-permute-done((bf16[32,1536]{1,0:T(8,128)(2,1)S(1)}, bf16[32,1536]{1,0:T(8,128)(2,1)S(1)}, u32[]{:S(2)}, u32[]{:S(2)}) %collective-permute-start.21) | collective-permute-done | bytes 98336 | tf_op jit(solution)/shard_map/ppermute | solution.py:22
  77.4 2.1 %collective-permute-start.24 = (bf16[96,1536]{1,0:T(8,128)(2,1)S(1)}, bf16[96,1536]{1,0:T(8,128)(2,1)S(1)}, u32[]{:S(2)}, u32[]{:S(2)}) collective-permute-start(bf16[96,1536]{1,0:T(8,128)(2,1)S(1)} %get-tuple-element.105), channel_id=1, source_target_pairs={{0,224},{16,240},{32,64},{48,80},{64,32},{80,48},{96,128},{112,144... | collective-permute-start | bytes 884744 | tf_op jit(solution)/shard_map/ppermute | solution.py:22
  83.3 2.7 %d_w_down.1 = bf16[384,1536]{1,0:T(8,128)(2,1)} custom-call(bf16[384,384]{1,0:T(8,128)(2,1)S(1)} %get-tuple-element.114.refs_0_, bf16[256,384]{1,0:T(8,128)(2,1)S(1)} %get-tuple-element.115.refs_1_, bf16[256,384]{1,0:T(8,128)(2,1)S(1)} %get-tuple-element.116.refs_2_, bf16[128,384]{1,0:T(8,128)(2,1)S(1)} %get-tuple-element.117.refs_3_, ...), custom_call_target="tpu_custom_call" | custom-call | flops 1207959552 | bytes 5111808 | tf_op jit(solution)/shard_map/d_w_down/pallas_call | solution.py:45
  90.9 3.0 %collective-permute-start.37 = (bf16[64,1536]{1,0:T(8,128)(2,1)S(1)}, bf16[64,1536]{1,0:T(8,128)(2,1)S(1)}, u32[]{:S(2)}, u32[]{:S(2)}) collective-permute-start(bf16[64,1536]{1,0:T(8,128)(2,1)S(1)} %get-tuple-element.153), channel_id=1, source_target_pairs={{0,128},{16,144},{32,160},{48,176},{64,192},{80,208},{96,224},{112... | collective-permute-start | bytes 589832 | tf_op jit(solution)/shard_map/ppermute | solution.py:34
  94.0 3.1 %d_w_gate.1 = bf16[1536,384]{1,0:T(8,128)(2,1)} custom-call(bf16[384,1536]{1,0:T(8,128)(2,1)S(1)} %get-tuple-element.154.refs_0_, bf16[256,1536]{1,0:T(8,128)(2,1)S(1)} %get-tuple-element.155.refs_1_, bf16[256,1536]{1,0:T(8,128)(2,1)S(1)} %get-tuple-element.156.refs_2_, bf16[128,1536]{1,0:T(8,128)(2,1)S(1)} %get-tuple-element.157.refs_3_, ...), custom_call_target="tpu_custom_call" | custom-call | flops 1207959552 | bytes 5111808 | tf_op jit(solution)/shard_map/d_w_gate/pallas_call | solution.py:45
  99.5 3.1 %d_w_up.1 = bf16[1536,384]{1,0:T(8,128)(2,1)} custom-call(bf16[384,1536]{1,0:T(8,128)(2,1)S(1)} %get-tuple-element.154.refs_0_, bf16[256,1536]{1,0:T(8,128)(2,1)S(1)} %get-tuple-element.155.refs_1_, bf16[256,1536]{1,0:T(8,128)(2,1)S(1)} %get-tuple-element.156.refs_2_, bf16[128,1536]{1,0:T(8,128)(2,1)S(1)} %get-tuple-element.157.refs_3_, ...), custom_call_target="tpu_custom_call" | custom-call | flops 1207959552 | bytes 5111808 | tf_op jit(solution)/shard_map/d_w_up/pallas_call | solution.py:45
  102.6 2.5 %collective-permute-done.36.c_ref = bf16[64,1536]{1,0:T(8,128)(2,1)S(1)} collective-permute-done((bf16[64,1536]{1,0:T(8,128)(2,1)S(1)}, bf16[64,1536]{1,0:T(8,128)(2,1)S(1)}, u32[]{:S(2)}, u32[]{:S(2)}) %collective-permute-start.36) | collective-permute-done | bytes 196640 | tf_op jit(solution)/shard_map/ppermute | solution.py:26
  105.1 3.1 %collective-permute-done.34.a_ref = bf16[80,1536]{1,0:T(8,128)(2,1)S(1)} collective-permute-done((bf16[80,1536]{1,0:T(8,128)(2,1)S(1)}, bf16[80,1536]{1,0:T(8,128)(2,1)S(1)}, u32[]{:S(2)}, u32[]{:S(2)}) %collective-permute-start.34) | collective-permute-done | bytes 245792 | tf_op jit(solution)/shard_map/ppermute | solution.py:22
  109.4 16.4 %all-to-all-start.1 = ((bf16[16,64,96]{2,1,0:T(8,128)(2,1)}), bf16[16,64,96]{2,1,0:T(8,128)(2,1)S(1)}, u32[]{:S(2)}, u32[]{:S(2)}) async-start(bf16[16,64,96]{2,1,0:T(8,128)(2,1)} %get-tuple-element.170), calls=%async_computation.1 | async-start | bytes 524288 | tf_op jit(solution)/shard_map/all_to_all | solution.py:239
  127.4 4.7 %collective-permute-done.38.two_ref = f32[1,1536]{1,0:T(1,128)S(1)} collective-permute-done((f32[1,1536]{1,0:T(1,128)S(1)}, f32[1,1536]{1,0:T(1,128)S(1)}, u32[]{:S(2)}, u32[]{:S(2)}) %collective-permute-start.38) | collective-permute-done | bytes 6176 | tf_op jit(solution)/shard_map/ppermute | solution.py:34
  (91 shorter events, 37.0 us)
Async XLA Ops:
  0.6 11.5 %collective-permute-start.5 = (bf16[64,1536]{1,0:T(8,128)(2,1)}, bf16[64,1536]{1,0:T(8,128)(2,1)S(1)}, u32[]{:S(2)}, u32[]{:S(2)}) collective-permute-start(bf16[64,1536]{1,0:T(8,128)(2,1)} %bitcast.23), channel_id=1, source_target_pairs={{0,16},{16,0},{32,48},{48,32},{64,80},{80,64},{96,112},{112,96},{1... | collective-permute-start | bytes 589832 | tf_op jit(solution)/shard_map/ppermute | solution.py:26
  4.6 16.4 %all-to-all-start = ((bf16[16,64,96]{2,1,0:T(8,128)(2,1)}), bf16[16,64,96]{2,1,0:T(8,128)(2,1)}, u32[]{:S(2)}, u32[]{:S(2)}) async-start(bf16[16,64,96]{2,1,0:T(8,128)(2,1)} %split_heads.1), calls=%async_computation | async-start | bytes 524288 | tf_op jit(solution)/shard_map/all_to_all | solution.py:239
  14.4 22.3 %collective-permute-start.6 = (bf16[128,1536]{1,0:T(8,128)(2,1)}, bf16[128,1536]{1,0:T(8,128)(2,1)}, u32[]{:S(2)}, u32[]{:S(2)}) collective-permute-start(bf16[128,1536]{1,0:T(8,128)(2,1)} %join_two.1.refs_6_), channel_id=1, source_target_pairs={{0,32},{16,48},{32,0},{48,16},{64,96},{80,112},{96,64},{112,80},{1... | collective-permute-start | bytes 1179656 | tf_op jit(solution)/shard_map/ppermute | solution.py:22
  16.1 20.9 %collective-permute-start.7 = (bf16[128,1536]{1,0:T(8,128)(2,1)}, bf16[128,1536]{1,0:T(8,128)(2,1)}, u32[]{:S(2)}, u32[]{:S(2)}) collective-permute-start(bf16[128,1536]{1,0:T(8,128)(2,1)} %join_two.1.refs_6_), channel_id=1, source_target_pairs={{0,224},{16,240},{32,64},{48,80},{64,32},{80,48},{96,128},{112,144... | collective-permute-start | bytes 1179656 | tf_op jit(solution)/shard_map/ppermute | solution.py:22
  23.1 11.3 %collective-permute-start.3 = (bf16[64,1536]{1,0:T(8,128)(2,1)S(1)}, bf16[64,1536]{1,0:T(8,128)(2,1)S(1)}, u32[]{:S(2)}, u32[]{:S(2)}) collective-permute-start(bf16[64,1536]{1,0:T(8,128)(2,1)S(1)} %get-tuple-element.89.refs_0_), channel_id=1, source_target_pairs={{0,224},{16,240},{32,64},{48,80},{64,32},{80,48},{96,128},{112,144... | collective-permute-start | bytes 589832 | tf_op jit(solution)/shard_map/ppermute | solution.py:22
  28.8 8.5 %collective-permute-start = (bf16[64,1536]{1,0:T(8,128)(2,1)S(1)}, bf16[64,1536]{1,0:T(8,128)(2,1)S(1)}, u32[]{:S(2)}, u32[]{:S(2)}) collective-permute-start(bf16[64,1536]{1,0:T(8,128)(2,1)S(1)} %get-tuple-element.89.refs_0_), channel_id=1, source_target_pairs={{0,16},{16,0},{32,48},{48,32},{64,80},{80,64},{96,112},{112,96},{1... | collective-permute-start | bytes 589832 | tf_op jit(solution)/shard_map/ppermute | solution.py:26
  36.7 15.7 %collective-permute-start.17 = (bf16[128,1536]{1,0:T(8,128)(2,1)}, bf16[128,1536]{1,0:T(8,128)(2,1)S(1)}, u32[]{:S(2)}, u32[]{:S(2)}) collective-permute-start(bf16[128,1536]{1,0:T(8,128)(2,1)} %collective-permute-done.6.refs_7_), channel_id=1, source_target_pairs={{0,224},{16,240},{32,64},{48,80},{64,32},{80,48},{96,128},{112,144... | collective-permute-start | bytes 1179656 | tf_op jit(solution)/shard_map/ppermute | solution.py:22
  37.0 15.6 %collective-permute-start.16 = (bf16[128,1536]{1,0:T(8,128)(2,1)}, bf16[128,1536]{1,0:T(8,128)(2,1)S(1)}, u32[]{:S(2)}, u32[]{:S(2)}) collective-permute-start(bf16[128,1536]{1,0:T(8,128)(2,1)} %collective-permute-done.7.refs_8_), channel_id=1, source_target_pairs={{0,32},{16,48},{32,0},{48,16},{64,96},{80,112},{96,64},{112,80},{1... | collective-permute-start | bytes 1179656 | tf_op jit(solution)/shard_map/ppermute | solution.py:22
  40.1 12.3 %collective-permute-start.10 = (bf16[64,1536]{1,0:T(8,128)(2,1)S(1)}, bf16[64,1536]{1,0:T(8,128)(2,1)S(1)}, u32[]{:S(2)}, u32[]{:S(2)}) collective-permute-start(bf16[64,1536]{1,0:T(8,128)(2,1)S(1)} %collective-permute-done.9.refs_2_), channel_id=1, source_target_pairs={{0,32},{16,48},{32,0},{48,16},{64,96},{80,112},{96,64},{112,80},{1... | collective-permute-start | bytes 589832 | tf_op jit(solution)/shard_map/ppermute | solution.py:22
  42.1 13.0 %collective-permute-start.11 = (bf16[64,1536]{1,0:T(8,128)(2,1)S(1)}, bf16[64,1536]{1,0:T(8,128)(2,1)S(1)}, u32[]{:S(2)}, u32[]{:S(2)}) collective-permute-start(bf16[64,1536]{1,0:T(8,128)(2,1)S(1)} %collective-permute-done.8.refs_0_), channel_id=1, source_target_pairs={{0,224},{16,240},{32,64},{48,80},{64,32},{80,48},{96,128},{112,144... | collective-permute-start | bytes 589832 | tf_op jit(solution)/shard_map/ppermute | solution.py:22
  52.4 11.6 %collective-permute-start.19 = (bf16[128,1536]{1,0:T(8,128)(2,1)S(1)}, bf16[128,1536]{1,0:T(8,128)(2,1)S(1)}, u32[]{:S(2)}, u32[]{:S(2)}) collective-permute-start(bf16[128,1536]{1,0:T(8,128)(2,1)S(1)} %collective-permute-done.17.refs_5_), channel_id=1, source_target_pairs={{0,32},{16,48},{32,0},{48,16},{64,96},{80,112},{96,64},{112,80},{1... | collective-permute-start | bytes 1179656 | tf_op jit(solution)/shard_map/ppermute | solution.py:22
  52.7 15.4 %collective-permute-start.20 = (bf16[128,1536]{1,0:T(8,128)(2,1)S(1)}, bf16[128,1536]{1,0:T(8,128)(2,1)S(1)}, u32[]{:S(2)}, u32[]{:S(2)}) collective-permute-start(bf16[128,1536]{1,0:T(8,128)(2,1)S(1)} %collective-permute-done.16.refs_4_), channel_id=1, source_target_pairs={{0,224},{16,240},{32,64},{48,80},{64,32},{80,48},{96,128},{112,144... | collective-permute-start | bytes 1179656 | tf_op jit(solution)/shard_map/ppermute | solution.py:22
  56.9 11.1 %collective-permute-start.15 = (bf16[64,1536]{1,0:T(8,128)(2,1)S(1)}, bf16[64,1536]{1,0:T(8,128)(2,1)S(1)}, u32[]{:S(2)}, u32[]{:S(2)}) collective-permute-start(bf16[64,1536]{1,0:T(8,128)(2,1)S(1)} %collective-permute-done.11.refs_2_), channel_id=1, source_target_pairs={{0,16},{16,0},{32,48},{48,32},{64,80},{80,64},{96,112},{112,96},{1... | collective-permute-start | bytes 589832 | tf_op jit(solution)/shard_map/ppermute | solution.py:26
  56.9 11.1 %collective-permute-start.18 = (bf16[64,1536]{1,0:T(8,128)(2,1)S(1)}, bf16[64,1536]{1,0:T(8,128)(2,1)S(1)}, u32[]{:S(2)}, u32[]{:S(2)}) collective-permute-start(bf16[64,1536]{1,0:T(8,128)(2,1)S(1)} %collective-permute-done.11.refs_2_), channel_id=1, source_target_pairs={{0,32},{16,48},{32,0},{48,16},{64,96},{80,112},{96,64},{112,80},{1... | collective-permute-start | bytes 589832 | tf_op jit(solution)/shard_map/ppermute | solution.py:22
  57.9 10.1 %collective-permute-start.14 = (bf16[64,1536]{1,0:T(8,128)(2,1)S(1)}, bf16[64,1536]{1,0:T(8,128)(2,1)S(1)}, u32[]{:S(2)}, u32[]{:S(2)}) collective-permute-start(bf16[64,1536]{1,0:T(8,128)(2,1)S(1)} %collective-permute-done.10.refs_0_), channel_id=1, source_target_pairs={{0,16},{16,0},{32,48},{48,32},{64,80},{80,64},{96,112},{112,96},{1... | collective-permute-start | bytes 589832 | tf_op jit(solution)/shard_map/ppermute | solution.py:26
  64.1 15.5 %collective-permute-start.28 = (bf16[128,1536]{1,0:T(8,128)(2,1)S(1)}, bf16[128,1536]{1,0:T(8,128)(2,1)S(1)}, u32[]{:S(2)}, u32[]{:S(2)}) collective-permute-start(bf16[128,1536]{1,0:T(8,128)(2,1)S(1)} %collective-permute-done.19.refs_4_), channel_id=1, source_target_pairs={{0,224},{16,240},{32,64},{48,80},{64,32},{80,48},{96,128},{112,144... | collective-permute-start | bytes 1179656 | tf_op jit(solution)/shard_map/ppermute | solution.py:22
  70.6 9.0 %collective-permute-start.27 = (bf16[64,1536]{1,0:T(8,128)(2,1)S(1)}, bf16[64,1536]{1,0:T(8,128)(2,1)S(1)}, u32[]{:S(2)}, u32[]{:S(2)}) collective-permute-start(bf16[64,1536]{1,0:T(8,128)(2,1)S(1)} %collective-permute-done.18.refs_0_), channel_id=1, source_target_pairs={{0,16},{16,0},{32,48},{48,32},{64,80},{80,64},{96,112},{112,96},{1... | collective-permute-start | bytes 589832 | tf_op jit(solution)/shard_map/ppermute | solution.py:26
  77.2 8.7 %collective-permute-start.26 = (bf16[64,1536]{1,0:T(8,128)(2,1)S(1)}, bf16[64,1536]{1,0:T(8,128)(2,1)S(1)}, u32[]{:S(2)}, u32[]{:S(2)}) collective-permute-start(bf16[64,1536]{1,0:T(8,128)(2,1)S(1)} %get-tuple-element.107), channel_id=1, source_target_pairs={{0,16},{16,0},{32,48},{48,32},{64,80},{80,64},{96,112},{112,96},{1... | collective-permute-start | bytes 589832 | tf_op jit(solution)/shard_map/ppermute | solution.py:26
  77.4 9.9 %collective-permute-start.24 = (bf16[96,1536]{1,0:T(8,128)(2,1)S(1)}, bf16[96,1536]{1,0:T(8,128)(2,1)S(1)}, u32[]{:S(2)}, u32[]{:S(2)}) collective-permute-start(bf16[96,1536]{1,0:T(8,128)(2,1)S(1)} %get-tuple-element.105), channel_id=1, source_target_pairs={{0,224},{16,240},{32,64},{48,80},{64,32},{80,48},{96,128},{112,144... | collective-permute-start | bytes 884744 | tf_op jit(solution)/shard_map/ppermute | solution.py:22
  87.6 9.5 %collective-permute-start.31 = (bf16[112,1536]{1,0:T(8,128)(2,1)S(1)}, bf16[112,1536]{1,0:T(8,128)(2,1)S(1)}, u32[]{:S(2)}, u32[]{:S(2)}) collective-permute-start(bf16[112,1536]{1,0:T(8,128)(2,1)S(1)} %get-tuple-element.129), channel_id=1, source_target_pairs={{0,224},{16,240},{32,64},{48,80},{64,32},{80,48},{96,128},{112,144... | collective-permute-start | bytes 1032200 | tf_op jit(solution)/shard_map/ppermute | solution.py:22
  90.9 8.6 %collective-permute-start.37 = (bf16[64,1536]{1,0:T(8,128)(2,1)S(1)}, bf16[64,1536]{1,0:T(8,128)(2,1)S(1)}, u32[]{:S(2)}, u32[]{:S(2)}) collective-permute-start(bf16[64,1536]{1,0:T(8,128)(2,1)S(1)} %get-tuple-element.153), channel_id=1, source_target_pairs={{0,128},{16,144},{32,160},{48,176},{64,192},{80,208},{96,224},{112... | collective-permute-start | bytes 589832 | tf_op jit(solution)/shard_map/ppermute | solution.py:34
  97.2 11.0 %collective-permute-start.34 = (bf16[80,1536]{1,0:T(8,128)(2,1)S(1)}, bf16[80,1536]{1,0:T(8,128)(2,1)S(1)}, u32[]{:S(2)}, u32[]{:S(2)}) collective-permute-start(bf16[80,1536]{1,0:T(8,128)(2,1)S(1)} %get-tuple-element.150), channel_id=1, source_target_pairs={{0,224},{16,240},{32,64},{48,80},{64,32},{80,48},{96,128},{112,144... | collective-permute-start | bytes 737288 | tf_op jit(solution)/shard_map/ppermute | solution.py:22
  98.3 9.9 %collective-permute-start.35 = (bf16[80,1536]{1,0:T(8,128)(2,1)S(1)}, bf16[80,1536]{1,0:T(8,128)(2,1)S(1)}, u32[]{:S(2)}, u32[]{:S(2)}) collective-permute-start(bf16[80,1536]{1,0:T(8,128)(2,1)S(1)} %get-tuple-element.151), channel_id=1, source_target_pairs={{0,32},{16,48},{32,0},{48,16},{64,96},{80,112},{96,64},{112,80},{1... | collective-permute-start | bytes 737288 | tf_op jit(solution)/shard_map/ppermute | solution.py:22
  109.4 25.1 %all-to-all-start.1 = ((bf16[16,64,96]{2,1,0:T(8,128)(2,1)}), bf16[16,64,96]{2,1,0:T(8,128)(2,1)S(1)}, u32[]{:S(2)}, u32[]{:S(2)}) async-start(bf16[16,64,96]{2,1,0:T(8,128)(2,1)} %get-tuple-element.170), calls=%async_computation.1 | async-start | bytes 524288 | tf_op jit(solution)/shard_map/all_to_all | solution.py:239
  (25 other events, 257.4 us)
where the time goes:
time: 136 us; the launch traced here: 135 us
  starting transfers between devices  68.2 us (50%)
  waiting for transfers between devices  37 us (27%)
  Pallas kernels  26.4 us (19%)
  local copies, waits for them, and re-layouts  2.8 us (2%)
    ppermute x22, starting transfers between devices, swap(): return lambda block: lax.ppermute(block, 'dp', pairs)  31.7 us
    pallas_call x16, Pallas kernels, kernel(): pl.pallas_call(body, out_shape=outs, in_specs=[whole] * len(args) if spec...  26.4 us
    all_to_all x2, starting transfers between devices, exchange(): lax.all_to_all(blocks, 'token', split_axis=0, concat_axis=0, tiled=True)  24 us
    ppermute x22, waiting for transfers between devices, swap(): return lambda block: lax.ppermute(block, 'dp', pairs)  21.3 us
    ppermute x15, waiting for transfers between devices, moves(): lax.ppermute(block, 'dp', [(at, at ^ 1) for at in range(size)])  9 us
    ppermute x15, starting transfers between devices, moves(): lax.ppermute(block, 'dp', [(at, at ^ 1) for at in range(size)])  7.73 us
    ppermute x2, waiting for transfers between devices, opposite(): lax.ppermute(block, 'dp', [(at, (at + size // 2) % size) for at in range(...  4.79 us
    ppermute x2, starting transfers between devices, opposite(): lax.ppermute(block, 'dp', [(at, (at + size // 2) % size) for at in range(...  4.72 us
  transfers between devices with their start and end apart: 41, of which 15 were waited for; matrix products, arithmetic and copies ran while one was open for 0% of the time, Pallas kernels for 18%

commit v1 on v0

--- a/solution.py
+++ b/solution.py
@@ -249,11 +249,12 @@
     u2, d2, s_u1, s_d1 = first(d1), other(u1), pair(u1), pair(d1)
     g_u2, g_d2 = first(g_d1), other(g_u1)
     u2, d2 = tie([u2, d2], [s0])
-    u3, d3, s_u2, s_d2 = first(d2), other(u2), pair(u2), pair(d2)
+    u3, d3 = first(d2), other(u2)
+    u2, d2 = tie([u2, d2], [s_u1, s_d1])
+    s_u2, s_d2 = pair(u2), pair(d2)
     g_u3, g_d3 = first(g_d2), other(g_u2)
-    u3, d3 = tie([u3, d3], [s_u1, s_d1, s_u2, s_d2])
-    s_u3, s_d3, far = pair(u3), pair(d3), first(d3)
-    g_far = other(g_u3)
+    s_u3, s_d3, far = pair(u3), pair(d3), other(u3)
+    g_far = first(g_d3)
     near = feed_forward([(hidden_in, s0), (u1, s_u1), (d1, s_d1)], [g0, g_u1, g_d1], w_gate, w_up, w_down)
     second = feed_forward([(u2, s_u2), (d2, s_d2)], [g_u2, g_d2], w_gate, w_up, w_down)
     s_u3, s_d3 = tie([s_u3, s_d3], [near[6], second[6], far])

time: 136 us -> 133 us (0.978)
  waiting for transfers between devices: 37 us -> 35 us
    ppermute x22, waiting for transfers between devices: 21.3 us -> 16 us  [swap(): return lambda block: lax.ppermute(block, 'dp', pairs)]
    ppermute x22, starting transfers between devices: 31.7 us -> 28.9 us  [swap(): return lambda block: lax.ppermute(block, 'dp', pairs)]
    ppermute x15, waiting for transfers between devices: 9 us -> 11.8 us  [moves(): lax.ppermute(block, 'dp', [(at, at ^ 1) for at in range(size)])]
    ppermute x15, starting transfers between devices: 7.73 us -> 10.2 us  [moves(): lax.ppermute(block, 'dp', [(at, at ^ 1) for at in range(size)])]
where the time goes in v1:
time: 133 us
  starting transfers between devices  67.9 us (51%)
  waiting for transfers between devices  35 us (26%)
  Pallas kernels  26.4 us (20%)
  local copies, waits for them, and re-layouts  2.8 us (2%)
    ppermute x22, starting transfers between devices, swap(): return lambda block: lax.ppermute(block, 'dp', pairs)  28.9 us
    pallas_call x16, Pallas kernels, kernel(): pl.pallas_call(body, out_shape=outs, in_specs=[whole] * len(args) if spec...  26.4 us
    all_to_all x2, starting transfers between devices, exchange(): lax.all_to_all(blocks, 'token', split_axis=0, concat_axis=0, tiled=True)  23.8 us
    ppermute x22, waiting for transfers between devices, swap(): return lambda block: lax.ppermute(block, 'dp', pairs)  16 us
    ppermute x15, waiting for transfers between devices, moves(): lax.ppermute(block, 'dp', [(at, at ^ 1) for at in range(size)])  11.8 us
    ppermute x15, starting transfers between devices, moves(): lax.ppermute(block, 'dp', [(at, at ^ 1) for at in range(size)])  10.2 us
    ppermute x2, waiting for transfers between devices, opposite(): lax.ppermute(block, 'dp', [(at, (at + size // 2) % size) for at in range(...  5.36 us
    ppermute x2, starting transfers between devices, opposite(): lax.ppermute(block, 'dp', [(at, (at + size // 2) % size) for at in range(...  5.03 us
  transfers between devices with their start and end apart: 41, of which 15 were waited for; matrix products, arithmetic and copies ran while one was open for 0% of the time, Pallas kernels for 18%

profile of v1, /device:TPU:1, one launch (start us, length us, event | category | flops | bytes accessed | tf_op | source)
XLA Modules:
  0.0 133.0 jit_solution(16494365167703718295)
XLA Ops:
  0.6 2.1 %collective-permute-start.5 = (bf16[64,1536]{1,0:T(8,128)(2,1)}, bf16[64,1536]{1,0:T(8,128)(2,1)S(1)}, u32[]{:S(2)}, u32[]{:S(2)}) collective-permute-start(bf16[64,1536]{1,0:T(8,128)(2,1)} %bitcast.23), channel_id=1, source_target_pairs={{0,16},{16,0},{32,48},{48,32},{64,80},{80,64},{96,112},{112,96},{1... | collective-permute-start | bytes 589832 | tf_op jit(solution)/shard_map/ppermute | solution.py:26
  4.6 7.6 %all-to-all-start = ((bf16[16,64,96]{2,1,0:T(8,128)(2,1)}), bf16[16,64,96]{2,1,0:T(8,128)(2,1)}, u32[]{:S(2)}, u32[]{:S(2)}) async-start(bf16[16,64,96]{2,1,0:T(8,128)(2,1)} %split_heads.1), calls=%async_computation | async-start | bytes 524288 | tf_op jit(solution)/shard_map/all_to_all | solution.py:239
  16.1 4.7 %collective-permute-start.7 = (bf16[128,1536]{1,0:T(8,128)(2,1)}, bf16[128,1536]{1,0:T(8,128)(2,1)}, u32[]{:S(2)}, u32[]{:S(2)}) collective-permute-start(bf16[128,1536]{1,0:T(8,128)(2,1)} %join_two.1.refs_6_), channel_id=1, source_target_pairs={{0,224},{16,240},{32,64},{48,80},{64,32},{80,48},{96,128},{112,144... | collective-permute-start | bytes 1179656 | tf_op jit(solution)/shard_map/ppermute | solution.py:22
  23.1 5.7 %collective-permute-start.3 = (bf16[64,1536]{1,0:T(8,128)(2,1)S(1)}, bf16[64,1536]{1,0:T(8,128)(2,1)S(1)}, u32[]{:S(2)}, u32[]{:S(2)}) collective-permute-start(bf16[64,1536]{1,0:T(8,128)(2,1)S(1)} %get-tuple-element.89.refs_0_), channel_id=1, source_target_pairs={{0,224},{16,240},{32,64},{48,80},{64,32},{80,48},{96,128},{112,144... | collective-permute-start | bytes 589832 | tf_op jit(solution)/shard_map/ppermute | solution.py:22
  28.8 5.6 %collective-permute-done.3.refs_4_ = bf16[64,1536]{1,0:T(8,128)(2,1)S(1)} collective-permute-done((bf16[64,1536]{1,0:T(8,128)(2,1)S(1)}, bf16[64,1536]{1,0:T(8,128)(2,1)S(1)}, u32[]{:S(2)}, u32[]{:S(2)}) %collective-permute-start.3) | collective-permute-done | bytes 196640 | tf_op jit(solution)/shard_map/ppermute | solution.py:22
  34.4 2.4 %collective-permute-start.9 = (bf16[64,1536]{1,0:T(8,128)(2,1)S(1)}, bf16[64,1536]{1,0:T(8,128)(2,1)S(1)}, u32[]{:S(2)}, u32[]{:S(2)}) collective-permute-start(bf16[64,1536]{1,0:T(8,128)(2,1)S(1)} %collective-permute-done.1.refs_2_), channel_id=1, source_target_pairs={{0,224},{16,240},{32,64},{48,80},{64,32},{80,48},{96,128},{112,144... | collective-permute-start | bytes 589832 | tf_op jit(solution)/shard_map/ppermute | solution.py:22
  36.7 2.2 %collective-permute-start.17 = (bf16[128,1536]{1,0:T(8,128)(2,1)}, bf16[128,1536]{1,0:T(8,128)(2,1)S(1)}, u32[]{:S(2)}, u32[]{:S(2)}) collective-permute-start(bf16[128,1536]{1,0:T(8,128)(2,1)} %collective-permute-done.6.refs_7_), channel_id=1, source_target_pairs={{0,224},{16,240},{32,64},{48,80},{64,32},{80,48},{96,128},{112,144... | collective-permute-start | bytes 1179656 | tf_op jit(solution)/shard_map/ppermute | solution.py:22
  41.0 2.8 %collective-permute-done.2.refs_3_ = bf16[64,1536]{1,0:T(8,128)(2,1)S(1)} collective-permute-done((bf16[64,1536]{1,0:T(8,128)(2,1)S(1)}, bf16[64,1536]{1,0:T(8,128)(2,1)S(1)}, u32[]{:S(2)}, u32[]{:S(2)}) %collective-permute-start.2) | collective-permute-done | bytes 196640 | tf_op jit(solution)/shard_map/ppermute | solution.py:26
  44.3 2.9 %collective-permute-done.4.refs_5_ = bf16[64,1536]{1,0:T(8,128)(2,1)S(1)} collective-permute-done((bf16[64,1536]{1,0:T(8,128)(2,1)S(1)}, bf16[64,1536]{1,0:T(8,128)(2,1)S(1)}, u32[]{:S(2)}, u32[]{:S(2)}) %collective-permute-start.4) | collective-permute-done | bytes 196640 | tf_op jit(solution)/shard_map/ppermute | solution.py:26
  47.3 5.2 %collective-permute-done.10.refs_0_ = bf16[64,1536]{1,0:T(8,128)(2,1)S(1)} collective-permute-done((bf16[64,1536]{1,0:T(8,128)(2,1)S(1)}, bf16[64,1536]{1,0:T(8,128)(2,1)S(1)}, u32[]{:S(2)}, u32[]{:S(2)}) %collective-permute-start.10) | collective-permute-done | bytes 196640 | tf_op jit(solution)/shard_map/ppermute | solution.py:22
  52.4 2.1 %collective-permute-start.20 = (bf16[128,1536]{1,0:T(8,128)(2,1)S(1)}, bf16[128,1536]{1,0:T(8,128)(2,1)S(1)}, u32[]{:S(2)}, u32[]{:S(2)}) collective-permute-start(bf16[128,1536]{1,0:T(8,128)(2,1)S(1)} %collective-permute-done.16.refs_4_), channel_id=1, source_target_pairs={{0,224},{16,240},{32,64},{48,80},{64,32},{80,48},{96,128},{112,144... | collective-permute-start | bytes 1179656 | tf_op jit(solution)/shard_map/ppermute | solution.py:22
  58.4 4.7 %feed_forward.4 = (bf16[384,1536]{1,0:T(8,128)(2,1)S(1)}, bf16[384,1536]{1,0:T(8,128)(2,1)S(1)}, bf16[384,384]{1,0:T(8,128)(2,1)S(1)}, bf16[384,384]{1,0:T(8,128...) custom-call(bf16[64,1536]{1,0:T(8,128)(2,1)S(1)} %get-tuple-element., ...), custom_call_target="tpu_custom_call" | custom-call | flops 2264924160 | bytes 10328064 | tf_op jit(solution)/shard_map/feed_forward/pallas_call | solution.py:45
  63.1 2.3 %feed_forward.5 = (bf16[256,1536]{1,0:T(8,128)(2,1)S(1)}, bf16[256,1536]{1,0:T(8,128)(2,1)S(1)}, bf16[256,384]{1,0:T(8,128)(2,1)S(1)}, bf16[256,384]{1,0:T(8,128...) custom-call(bf16[64,1536]{1,0:T(8,128)(2,1)S(1)} %collective-permute, ...), custom_call_target="tpu_custom_call" | custom-call | flops 1509949440 | bytes 8067072 | tf_op jit(solution)/shard_map/feed_forward/pallas_call | solution.py:45
  66.8 2.3 %feed_forward.6 = (bf16[256,1536]{1,0:T(8,128)(2,1)S(1)}, bf16[256,1536]{1,0:T(8,128)(2,1)S(1)}, bf16[256,384]{1,0:T(8,128)(2,1)S(1)}, bf16[256,384]{1,0:T(8,128...) custom-call(bf16[64,1536]{1,0:T(8,128)(2,1)S(1)} %collective-permute, ...), custom_call_target="tpu_custom_call" | custom-call | flops 1509949440 | bytes 8067072 | tf_op jit(solution)/shard_map/feed_forward/pallas_call | solution.py:45
  72.1 3.2 %collective-permute-done.21.refs_0_ = bf16[32,1536]{1,0:T(8,128)(2,1)S(1)} collective-permute-done((bf16[32,1536]{1,0:T(8,128)(2,1)S(1)}, bf16[32,1536]{1,0:T(8,128)(2,1)S(1)}, u32[]{:S(2)}, u32[]{:S(2)}) %collective-permute-start.21) | collective-permute-done | bytes 98336 | tf_op jit(solution)/shard_map/ppermute | solution.py:22
  82.1 2.7 %d_w_down.1 = bf16[384,1536]{1,0:T(8,128)(2,1)} custom-call(bf16[384,384]{1,0:T(8,128)(2,1)S(1)} %get-tuple-element.114.refs_0_, bf16[256,384]{1,0:T(8,128)(2,1)S(1)} %get-tuple-element.115.refs_1_, bf16[256,384]{1,0:T(8,128)(2,1)S(1)} %get-tuple-element.116.refs_2_, bf16[128,384]{1,0:T(8,128)(2,1)S(1)} %get-tuple-element.117.refs_3_, ...), custom_call_target="tpu_custom_call" | custom-call | flops 1207959552 | bytes 5111808 | tf_op jit(solution)/shard_map/d_w_down/pallas_call | solution.py:45
  84.8 2.5 %collective-permute-done.29.refs_10_.refs_7_ = f32[1,1536]{1,0:T(1,128)S(1)} collective-permute-done((f32[1,1536]{1,0:T(1,128)S(1)}, f32[1,1536]{1,0:T(1,128)S(1)}, u32[]{:S(2)}, u32[]{:S(2)}) %collective-permute-start.29) | collective-permute-done | bytes 6176 | tf_op jit(solution)/shard_map/ppermute | solution.py:26
  87.7 2.3 %collective-permute-start.32 = (bf16[112,1536]{1,0:T(8,128)(2,1)S(1)}, bf16[112,1536]{1,0:T(8,128)(2,1)S(1)}, u32[]{:S(2)}, u32[]{:S(2)}) collective-permute-start(bf16[112,1536]{1,0:T(8,128)(2,1)S(1)} %get-tuple-element.130), channel_id=1, source_target_pairs={{0,32},{16,48},{32,0},{48,16},{64,96},{80,112},{96,64},{112,80},{1... | collective-permute-start | bytes 1032200 | tf_op jit(solution)/shard_map/ppermute | solution.py:22
  92.8 3.1 %d_w_gate.1 = bf16[1536,384]{1,0:T(8,128)(2,1)} custom-call(bf16[384,1536]{1,0:T(8,128)(2,1)S(1)} %get-tuple-element.154.refs_0_, bf16[256,1536]{1,0:T(8,128)(2,1)S(1)} %get-tuple-element.155.refs_1_, bf16[256,1536]{1,0:T(8,128)(2,1)S(1)} %get-tuple-element.156.refs_2_, bf16[128,1536]{1,0:T(8,128)(2,1)S(1)} %get-tuple-element.157.refs_3_, ...), custom_call_target="tpu_custom_call" | custom-call | flops 1207959552 | bytes 5111808 | tf_op jit(solution)/shard_map/d_w_gate/pallas_call | solution.py:45
  96.1 2.2 %collective-permute-start.34 = (bf16[80,1536]{1,0:T(8,128)(2,1)S(1)}, bf16[80,1536]{1,0:T(8,128)(2,1)S(1)}, u32[]{:S(2)}, u32[]{:S(2)}) collective-permute-start(bf16[80,1536]{1,0:T(8,128)(2,1)S(1)} %get-tuple-element.150), channel_id=1, source_target_pairs={{0,224},{16,240},{32,64},{48,80},{64,32},{80,48},{96,128},{112,144... | collective-permute-start | bytes 737288 | tf_op jit(solution)/shard_map/ppermute | solution.py:22
  101.0 3.1 %d_w_up.1 = bf16[1536,384]{1,0:T(8,128)(2,1)} custom-call(bf16[384,1536]{1,0:T(8,128)(2,1)S(1)} %get-tuple-element.154.refs_0_, bf16[256,1536]{1,0:T(8,128)(2,1)S(1)} %get-tuple-element.155.refs_1_, bf16[256,1536]{1,0:T(8,128)(2,1)S(1)} %get-tuple-element.156.refs_2_, bf16[128,1536]{1,0:T(8,128)(2,1)S(1)} %get-tuple-element.157.refs_3_, ...), custom_call_target="tpu_custom_call" | custom-call | flops 1207959552 | bytes 5111808 | tf_op jit(solution)/shard_map/d_w_up/pallas_call | solution.py:45
  107.4 16.2 %all-to-all-start.1 = ((bf16[16,64,96]{2,1,0:T(8,128)(2,1)}), bf16[16,64,96]{2,1,0:T(8,128)(2,1)S(1)}, u32[]{:S(2)}, u32[]{:S(2)}) async-start(bf16[16,64,96]{2,1,0:T(8,128)(2,1)} %get-tuple-element.170), calls=%async_computation.1 | async-start | bytes 524288 | tf_op jit(solution)/shard_map/all_to_all | solution.py:239
  123.6 3.1 %collective-permute-start.38 = (f32[1,1536]{1,0:T(1,128)S(1)}, f32[1,1536]{1,0:T(1,128)S(1)}, u32[]{:S(2)}, u32[]{:S(2)}) collective-permute-start(f32[1,1536]{1,0:T(1,128)S(1)} %get-tuple-element.172.near_ref), channel_id=1, source_target_pairs={{0,128},{16,144},{32,160},{48,176},{64,192},{80,208},{96,224},{112... | collective-permute-start | bytes 18440 | tf_op jit(solution)/shard_map/ppermute | solution.py:34
  126.7 3.3 %collective-permute-done.38.two_ref = f32[1,1536]{1,0:T(1,128)S(1)} collective-permute-done((f32[1,1536]{1,0:T(1,128)S(1)}, f32[1,1536]{1,0:T(1,128)S(1)}, u32[]{:S(2)}, u32[]{:S(2)}) %collective-permute-start.38) | collective-permute-done | bytes 6176 | tf_op jit(solution)/shard_map/ppermute | solution.py:34
  (91 shorter events, 38.0 us)
Async XLA Ops:
  0.6 11.5 %collective-permute-start.5 = (bf16[64,1536]{1,0:T(8,128)(2,1)}, bf16[64,1536]{1,0:T(8,128)(2,1)S(1)}, u32[]{:S(2)}, u32[]{:S(2)}) collective-permute-start(bf16[64,1536]{1,0:T(8,128)(2,1)} %bitcast.23), channel_id=1, source_target_pairs={{0,16},{16,0},{32,48},{48,32},{64,80},{80,64},{96,112},{112,96},{1... | collective-permute-start | bytes 589832 | tf_op jit(solution)/shard_map/ppermute | solution.py:26
  4.6 16.4 %all-to-all-start = ((bf16[16,64,96]{2,1,0:T(8,128)(2,1)}), bf16[16,64,96]{2,1,0:T(8,128)(2,1)}, u32[]{:S(2)}, u32[]{:S(2)}) async-start(bf16[16,64,96]{2,1,0:T(8,128)(2,1)} %split_heads.1), calls=%async_computation | async-start | bytes 524288 | tf_op jit(solution)/shard_map/all_to_all | solution.py:239
  14.4 22.3 %collective-permute-start.6 = (bf16[128,1536]{1,0:T(8,128)(2,1)}, bf16[128,1536]{1,0:T(8,128)(2,1)}, u32[]{:S(2)}, u32[]{:S(2)}) collective-permute-start(bf16[128,1536]{1,0:T(8,128)(2,1)} %join_two.1.refs_6_), channel_id=1, source_target_pairs={{0,32},{16,48},{32,0},{48,16},{64,96},{80,112},{96,64},{112,80},{1... | collective-permute-start | bytes 1179656 | tf_op jit(solution)/shard_map/ppermute | solution.py:22
  16.1 20.6 %collective-permute-start.7 = (bf16[128,1536]{1,0:T(8,128)(2,1)}, bf16[128,1536]{1,0:T(8,128)(2,1)}, u32[]{:S(2)}, u32[]{:S(2)}) collective-permute-start(bf16[128,1536]{1,0:T(8,128)(2,1)} %join_two.1.refs_6_), channel_id=1, source_target_pairs={{0,224},{16,240},{32,64},{48,80},{64,32},{80,48},{96,128},{112,144... | collective-permute-start | bytes 1179656 | tf_op jit(solution)/shard_map/ppermute | solution.py:22
  23.1 11.3 %collective-permute-start.3 = (bf16[64,1536]{1,0:T(8,128)(2,1)S(1)}, bf16[64,1536]{1,0:T(8,128)(2,1)S(1)}, u32[]{:S(2)}, u32[]{:S(2)}) collective-permute-start(bf16[64,1536]{1,0:T(8,128)(2,1)S(1)} %get-tuple-element.89.refs_0_), channel_id=1, source_target_pairs={{0,224},{16,240},{32,64},{48,80},{64,32},{80,48},{96,128},{112,144... | collective-permute-start | bytes 589832 | tf_op jit(solution)/shard_map/ppermute | solution.py:22
  28.8 10.2 %collective-permute-start = (bf16[64,1536]{1,0:T(8,128)(2,1)S(1)}, bf16[64,1536]{1,0:T(8,128)(2,1)S(1)}, u32[]{:S(2)}, u32[]{:S(2)}) collective-permute-start(bf16[64,1536]{1,0:T(8,128)(2,1)S(1)} %get-tuple-element.89.refs_0_), channel_id=1, source_target_pairs={{0,16},{16,0},{32,48},{48,32},{64,80},{80,64},{96,112},{112,96},{1... | collective-permute-start | bytes 589832 | tf_op jit(solution)/shard_map/ppermute | solution.py:26
  36.7 15.7 %collective-permute-start.16 = (bf16[128,1536]{1,0:T(8,128)(2,1)}, bf16[128,1536]{1,0:T(8,128)(2,1)S(1)}, u32[]{:S(2)}, u32[]{:S(2)}) collective-permute-start(bf16[128,1536]{1,0:T(8,128)(2,1)} %collective-permute-done.7.refs_8_), channel_id=1, source_target_pairs={{0,32},{16,48},{32,0},{48,16},{64,96},{80,112},{96,64},{112,80},{1... | collective-permute-start | bytes 1179656 | tf_op jit(solution)/shard_map/ppermute | solution.py:22
  36.7 17.8 %collective-permute-start.17 = (bf16[128,1536]{1,0:T(8,128)(2,1)}, bf16[128,1536]{1,0:T(8,128)(2,1)S(1)}, u32[]{:S(2)}, u32[]{:S(2)}) collective-permute-start(bf16[128,1536]{1,0:T(8,128)(2,1)} %collective-permute-done.6.refs_7_), channel_id=1, source_target_pairs={{0,224},{16,240},{32,64},{48,80},{64,32},{80,48},{96,128},{112,144... | collective-permute-start | bytes 1179656 | tf_op jit(solution)/shard_map/ppermute | solution.py:22
  40.4 12.0 %collective-permute-start.10 = (bf16[64,1536]{1,0:T(8,128)(2,1)S(1)}, bf16[64,1536]{1,0:T(8,128)(2,1)S(1)}, u32[]{:S(2)}, u32[]{:S(2)}) collective-permute-start(bf16[64,1536]{1,0:T(8,128)(2,1)S(1)} %collective-permute-done.9.refs_2_), channel_id=1, source_target_pairs={{0,32},{16,48},{32,0},{48,16},{64,96},{80,112},{96,64},{112,80},{1... | collective-permute-start | bytes 589832 | tf_op jit(solution)/shard_map/ppermute | solution.py:22
  43.8 10.8 %collective-permute-start.12 = (bf16[64,1536]{1,0:T(8,128)(2,1)S(1)}, bf16[64,1536]{1,0:T(8,128)(2,1)S(1)}, u32[]{:S(2)}, u32[]{:S(2)}) collective-permute-start(bf16[64,1536]{1,0:T(8,128)(2,1)S(1)} %collective-permute-done.8.refs_0_), channel_id=1, source_target_pairs={{0,224},{16,240},{32,64},{48,80},{64,32},{80,48},{96,128},{112,144... | collective-permute-start | bytes 589832 | tf_op jit(solution)/shard_map/ppermute | solution.py:22
  47.2 8.9 %collective-permute-start.14 = (bf16[64,1536]{1,0:T(8,128)(2,1)S(1)}, bf16[64,1536]{1,0:T(8,128)(2,1)S(1)}, u32[]{:S(2)}, u32[]{:S(2)}) collective-permute-start(bf16[64,1536]{1,0:T(8,128)(2,1)S(1)} %collective-permute-done.8.refs_0_), channel_id=1, source_target_pairs={{0,16},{16,0},{32,48},{48,32},{64,80},{80,64},{96,112},{112,96},{1... | collective-permute-start | bytes 589832 | tf_op jit(solution)/shard_map/ppermute | solution.py:26
  52.4 10.6 %collective-permute-start.20 = (bf16[128,1536]{1,0:T(8,128)(2,1)S(1)}, bf16[128,1536]{1,0:T(8,128)(2,1)S(1)}, u32[]{:S(2)}, u32[]{:S(2)}) collective-permute-start(bf16[128,1536]{1,0:T(8,128)(2,1)S(1)} %collective-permute-done.16.refs_4_), channel_id=1, source_target_pairs={{0,224},{16,240},{32,64},{48,80},{64,32},{80,48},{96,128},{112,144... | collective-permute-start | bytes 1179656 | tf_op jit(solution)/shard_map/ppermute | solution.py:22
  54.5 12.2 %collective-permute-start.19 = (bf16[128,1536]{1,0:T(8,128)(2,1)S(1)}, bf16[128,1536]{1,0:T(8,128)(2,1)S(1)}, u32[]{:S(2)}, u32[]{:S(2)}) collective-permute-start(bf16[128,1536]{1,0:T(8,128)(2,1)S(1)} %collective-permute-done.17.refs_5_), channel_id=1, source_target_pairs={{0,32},{16,48},{32,0},{48,16},{64,96},{80,112},{96,64},{112,80},{1... | collective-permute-start | bytes 1179656 | tf_op jit(solution)/shard_map/ppermute | solution.py:22
  54.5 10.9 %collective-permute-start.11 = (bf16[64,1536]{1,0:T(8,128)(2,1)S(1)}, bf16[64,1536]{1,0:T(8,128)(2,1)S(1)}, u32[]{:S(2)}, u32[]{:S(2)}) collective-permute-start(bf16[64,1536]{1,0:T(8,128)(2,1)S(1)} %collective-permute-done.10.refs_0_), channel_id=1, source_target_pairs={{0,16},{16,0},{32,48},{48,32},{64,80},{80,64},{96,112},{112,96},{1... | collective-permute-start | bytes 589832 | tf_op jit(solution)/shard_map/ppermute | solution.py:26
  56.1 10.7 %collective-permute-start.18 = (bf16[64,1536]{1,0:T(8,128)(2,1)S(1)}, bf16[64,1536]{1,0:T(8,128)(2,1)S(1)}, u32[]{:S(2)}, u32[]{:S(2)}) collective-permute-start(bf16[64,1536]{1,0:T(8,128)(2,1)S(1)} %collective-permute-done.10.refs_0_), channel_id=1, source_target_pairs={{0,224},{16,240},{32,64},{48,80},{64,32},{80,48},{96,128},{112,144... | collective-permute-start | bytes 589832 | tf_op jit(solution)/shard_map/ppermute | solution.py:22
  58.3 8.4 %collective-permute-start.13 = (bf16[64,1536]{1,0:T(8,128)(2,1)S(1)}, bf16[64,1536]{1,0:T(8,128)(2,1)S(1)}, u32[]{:S(2)}, u32[]{:S(2)}) collective-permute-start(bf16[64,1536]{1,0:T(8,128)(2,1)S(1)} %collective-permute-done.12.refs_2_), channel_id=1, source_target_pairs={{0,16},{16,0},{32,48},{48,32},{64,80},{80,64},{96,112},{112,96},{1... | collective-permute-start | bytes 589832 | tf_op jit(solution)/shard_map/ppermute | solution.py:26
  63.0 15.3 %collective-permute-start.28 = (bf16[128,1536]{1,0:T(8,128)(2,1)S(1)}, bf16[128,1536]{1,0:T(8,128)(2,1)S(1)}, u32[]{:S(2)}, u32[]{:S(2)}) collective-permute-start(bf16[128,1536]{1,0:T(8,128)(2,1)S(1)} %collective-permute-done.20.refs_5_), channel_id=1, source_target_pairs={{0,32},{16,48},{32,0},{48,16},{64,96},{80,112},{96,64},{112,80},{1... | collective-permute-start | bytes 1179656 | tf_op jit(solution)/shard_map/ppermute | solution.py:22
  75.3 9.5 %collective-permute-start.26 = (bf16[64,1536]{1,0:T(8,128)(2,1)S(1)}, bf16[64,1536]{1,0:T(8,128)(2,1)S(1)}, u32[]{:S(2)}, u32[]{:S(2)}) collective-permute-start(bf16[64,1536]{1,0:T(8,128)(2,1)S(1)} %get-tuple-element.107), channel_id=1, source_target_pairs={{0,16},{16,0},{32,48},{48,32},{64,80},{80,64},{96,112},{112,96},{1... | collective-permute-start | bytes 589832 | tf_op jit(solution)/shard_map/ppermute | solution.py:26
  76.5 10.9 %collective-permute-start.24 = (bf16[96,1536]{1,0:T(8,128)(2,1)S(1)}, bf16[96,1536]{1,0:T(8,128)(2,1)S(1)}, u32[]{:S(2)}, u32[]{:S(2)}) collective-permute-start(bf16[96,1536]{1,0:T(8,128)(2,1)S(1)} %get-tuple-element.105), channel_id=1, source_target_pairs={{0,224},{16,240},{32,64},{48,80},{64,32},{80,48},{96,128},{112,144... | collective-permute-start | bytes 884744 | tf_op jit(solution)/shard_map/ppermute | solution.py:22
  78.4 9.0 %collective-permute-start.25 = (bf16[96,1536]{1,0:T(8,128)(2,1)S(1)}, bf16[96,1536]{1,0:T(8,128)(2,1)S(1)}, u32[]{:S(2)}, u32[]{:S(2)}) collective-permute-start(bf16[96,1536]{1,0:T(8,128)(2,1)S(1)} %get-tuple-element.106), channel_id=1, source_target_pairs={{0,32},{16,48},{32,0},{48,16},{64,96},{80,112},{96,64},{112,80},{1... | collective-permute-start | bytes 884744 | tf_op jit(solution)/shard_map/ppermute | solution.py:22
  87.6 8.2 %collective-permute-start.31 = (bf16[112,1536]{1,0:T(8,128)(2,1)S(1)}, bf16[112,1536]{1,0:T(8,128)(2,1)S(1)}, u32[]{:S(2)}, u32[]{:S(2)}) collective-permute-start(bf16[112,1536]{1,0:T(8,128)(2,1)S(1)} %get-tuple-element.129), channel_id=1, source_target_pairs={{0,224},{16,240},{32,64},{48,80},{64,32},{80,48},{96,128},{112,144... | collective-permute-start | bytes 1032200 | tf_op jit(solution)/shard_map/ppermute | solution.py:22
  90.8 10.1 %collective-permute-start.37 = (bf16[64,1536]{1,0:T(8,128)(2,1)S(1)}, bf16[64,1536]{1,0:T(8,128)(2,1)S(1)}, u32[]{:S(2)}, u32[]{:S(2)}) collective-permute-start(bf16[64,1536]{1,0:T(8,128)(2,1)S(1)} %get-tuple-element.153), channel_id=1, source_target_pairs={{0,128},{16,144},{32,160},{48,176},{64,192},{80,208},{96,224},{112... | collective-permute-start | bytes 589832 | tf_op jit(solution)/shard_map/ppermute | solution.py:34
  96.1 10.1 %collective-permute-start.34 = (bf16[80,1536]{1,0:T(8,128)(2,1)S(1)}, bf16[80,1536]{1,0:T(8,128)(2,1)S(1)}, u32[]{:S(2)}, u32[]{:S(2)}) collective-permute-start(bf16[80,1536]{1,0:T(8,128)(2,1)S(1)} %get-tuple-element.150), channel_id=1, source_target_pairs={{0,224},{16,240},{32,64},{48,80},{64,32},{80,48},{96,128},{112,144... | collective-permute-start | bytes 737288 | tf_op jit(solution)/shard_map/ppermute | solution.py:22
  107.4 24.9 %all-to-all-start.1 = ((bf16[16,64,96]{2,1,0:T(8,128)(2,1)}), bf16[16,64,96]{2,1,0:T(8,128)(2,1)S(1)}, u32[]{:S(2)}, u32[]{:S(2)}) async-start(bf16[16,64,96]{2,1,0:T(8,128)(2,1)} %get-tuple-element.170), calls=%async_computation.1 | async-start | bytes 524288 | tf_op jit(solution)/shard_map/all_to_all | solution.py:239
  (25 other events, 255.3 us)
